TPU v7x, 32 devices: a whole 2x2x4 slice. The times are simulated.
32 devices in a mesh: row: 4 (over z), col: 8 (over y, x, core).
Axes of the slice: x: 2, y: 2, z: 4, core: 2. Of those that a mesh axis runs over, the one named last changes fastest.
Arguments:
- matrix_tiles: bfloat16 [4, 8, 384, 128, 128], P('row', 'col')
- row_coords: int32 [4, 8, 384], P('row', 'col'), may hold values from 0 to 2047, as said below
- col_coords: int32 [4, 8, 384], P('row', 'col'), may hold values from 0 to 1023, as said below
- left_basis: float32 [8, 8192, 128], P(None, ('row', 'col'))
- right_basis: float32 [8, 8192, 128], P(None, ('col', 'row'))
Outputs:
- new_left: float32 [2, 8192, 128], P(None, ('row', 'col'))
- new_right: float32 [2, 8192, 128], P(None, ('col', 'row'))
- bidiagonal: float32 [2, 2], replicated
Inputs may be any that keep to these rules, and one draw needn't show every extreme that they name: `row_coords`: slot s of a device lies in row blocks 256 * a to 256 * a + 255 of its row group, with a = s // 48. `col_coords`: slot s of a device lies in column blocks 256 * b to 256 * b + 255 of its column group, with b = (s // 12) % 4.
All inputs are finite; a program needn't handle non-finite values.
Results may differ from a plain program's by a relative error of at most 0.0012.
Values may be sent and summed in bfloat16 or wider, within the bound.
A program may use at most 64 MiB of HBM per device.

v0:
```python
import functools
import jax
import jax.numpy as jnp
from jax import lax
from jax.experimental import pallas as pl
from jax.experimental.pallas import tpu as pltpu
from jax.sharding import PartitionSpec as P

ITERS = 2
EPS = 1e-6
MESH = pl.DeviceIdType.MESH
NN = (((1,), (0,)), ((), ()))
NT = (((1,), (1,)), ((), ()))
F32 = jnp.float32
BF16 = jnp.bfloat16


def dot(a, b, dims=NN):
    return lax.dot_general(a, b, dims, preferred_element_type=F32)


def floor_div(x, n):
    return jnp.floor((x + 0.5) * (1.0 / n))


def kernel(
    n_rows, n_cols, slots, own, bs, kb,
    tiles, rc, cc, lb, rb,
    nl, nr, bd,
    a_v, idl_s, idl_r, idr_s, idr_r, gl, sl, gr, sr, pm, pmt,
    xs, xr, zs, zr, ps, pr, qs, qr, xp, tc_s, tc_r, tr_s, tr_r,
    a_sem, cs_sem, cr_sem, rs_sem, rr_sem,
):
    i = lax.axis_index("row")
    j = lax.axis_index("col")
    cl = slots // n_cols
    rl = slots // n_rows
    cell = slots // (n_rows * n_cols)
    inverse = 1.0 / (own * bs * n_rows * n_cols)

    def load(b):
        part = pl.ds(b * rl, rl)
        return pltpu.make_async_copy(tiles.at[0, 0, part], a_v.at[part], a_sem.at[b])

    for b in range(n_rows):
        load(b).start()

    barrier = pltpu.get_barrier_semaphore()
    for d in range(1, n_cols):
        pl.semaphore_signal(barrier, inc=1, device_id={"col": lax.rem(j + d, n_cols)}, device_id_type=MESH)
    for d in range(1, n_rows):
        pl.semaphore_signal(barrier, inc=1, device_id={"row": lax.rem(i + d, n_rows)}, device_id_type=MESH)

    sends = []
    axes = {"col": (j, n_cols, cs_sem, cr_sem), "row": (i, n_rows, rs_sem, rr_sem)}
    used = {"col": 0, "row": 0}

    def exchange(axis, src, dst):
        me, n, ssem, rsem = axes[axis]
        phase = used[axis]
        used[axis] += 1
        copies = []
        for d in range(1, n):
            peer = lax.rem(me + d, n)
            copy = pltpu.make_async_remote_copy(
                src_ref=src(peer), dst_ref=dst(me),
                send_sem=ssem.at[phase, d], recv_sem=rsem.at[phase, d],
                device_id={axis: peer}, device_id_type=MESH,
            )
            copy.start()
            sends.append(copy)
            copies.append(copy)

        def wait():
            for copy in copies:
                copy.wait_recv()
        return wait

    def rows_exchange(axis, src, dst):
        me = axes[axis][0]
        n = cl if axis == "col" else rl
        part = lambda ref: lambda p: ref.at[pl.ds(pl.multiple_of(p * n, n), n)]
        wait = exchange(axis, part(src), part(dst))
        mine = pl.ds(pl.multiple_of(me * n, n), n)
        dst[mine, :] = src[mine, :]
        return wait

    def place(s):
        a = floor_div(s, cl)
        q = floor_div(s, cell)
        b = q - n_rows * floor_div(q, n_rows)
        return b * rl + a * cell + (s - q * cell)

    it0 = lax.broadcasted_iota(jnp.int32, (slots, slots), 0).astype(F32)
    it1 = lax.broadcasted_iota(jnp.int32, (slots, slots), 1).astype(F32)
    pm[...] = jnp.where(place(it0) == it1, 1.0, 0.0).astype(BF16)
    pmt[...] = jnp.where(place(it1) == it0, 1.0, 0.0).astype(BF16)

    def column(row):
        return jnp.transpose(jnp.broadcast_to(row, (bs, slots)))

    lane = lax.broadcasted_iota(jnp.int32, (1, slots), 1).astype(F32)
    r_loc = rc[0, 0:1, :].astype(F32) - own * floor_div(lane, cl)
    q = floor_div(lane, cell)
    c_loc = cc[0, 0:1, :].astype(F32) - own * (q - n_rows * floor_div(q, n_rows))
    idl_s[...] = column(r_loc).astype(idl_s.dtype)
    idr_s[...] = dot(pmt[...], column(c_loc).astype(BF16)).astype(BF16)

    pl.semaphore_wait(barrier, n_cols + n_rows - 2)
    wait_r = rows_exchange("row", idr_s, idr_r)
    wait_l = rows_exchange("col", idl_s, idl_r)

    lane8 = lax.broadcasted_iota(jnp.int32, (kb, bs), 1)

    def lanes_to_column(rows):
        return jnp.sum(jnp.concatenate(rows, axis=0), axis=1, keepdims=True)

    def correlate(vectors, target):
        return lanes_to_column([jnp.sum(v[...] * target, axis=0, keepdims=True) for v in vectors])

    left = [lb.at[k] for k in range(kb)]
    right = [rb.at[k] for k in range(kb)]

    all_reduce_count = [0]

    def all_reduce(tile):
        n = all_reduce_count[0]
        all_reduce_count[0] += 1
        tc_s[n] = tile
        tc_r[n, j] = tile
        wait = exchange("col", lambda p: tc_s.at[n], lambda p: tc_r.at[n, p])

        def middle():
            wait()
            total = tc_r[n, 0]
            for k in range(1, n_cols):
                total = total + tc_r[n, k]
            tr_s[n] = total
            tr_r[n, i] = total
            wait2 = exchange("row", lambda p: tr_s.at[n], lambda p: tr_r.at[n, p])

            def final():
                wait2()
                total = tr_r[n, 0]
                for k in range(1, n_rows):
                    total = total + tr_r[n, k]
                return total * inverse
            return final
        return middle

    gram = jnp.zeros((kb, bs), F32)
    for side, vectors in enumerate((right, left)):
        for l in range(kb):
            col = correlate(vectors, vectors[l][...])
            gram = gram + jnp.where(lane8 == side * kb + l, col, 0.0)
        if side == 0:
            def one_hot(idx, g, s):
                halves = [
                    jnp.where(
                        idx[...].astype(F32)
                        == (lax.broadcasted_iota(jnp.int32, (slots, bs), 1) + h * bs).astype(F32),
                        1.0, 0.0)
                    for h in range(own // bs)
                ]
                whole = jnp.concatenate(halves, axis=1)
                g[...] = whole.astype(BF16)
                s[...] = jnp.transpose(whole).astype(BF16)

            wait_r()
            one_hot(idr_r, gr, sr)
            xs[0] = dot(gr[...], rb[kb - 1].astype(BF16)).astype(BF16)
            wait_x = rows_exchange("row", xs.at[0], xr.at[0])
    middle = all_reduce(gram)
    wait_l()
    one_hot(idl_r, gl, sl)
    final = middle()
    grams = None

    row16 = lax.broadcasted_iota(jnp.int32, (16, bs), 0)

    def products(x, out, transposed, first):
        def body(b, carry):
            if first:
                load(b).wait()
            for g in range(rl // 16):
                part = pl.ds(pl.multiple_of(b * rl + g * 16, 16), 16)
                xg = x[part, :].astype(F32)
                acc = jnp.zeros((16, bs), F32)
                for r in range(16):
                    one = jnp.where(row16 == r, xg, 0.0).astype(BF16)
                    k = g * 16 + r
                    if transposed:
                        t = k // cell * cl + b * cell + k % cell
                        acc = acc + dot(one, a_v[t], NN)
                    else:
                        acc = acc + dot(one, a_v[b * rl + k], NT)
                out[part, :] = acc
            return carry
        lax.fori_loop(0, n_rows, body, 0)

    def scatter(s, got):
        value = got[...]
        high = value.astype(BF16)
        rest = value - high.astype(F32)
        mid = rest.astype(BF16)
        low = (rest - mid.astype(F32)).astype(BF16)
        return dot(s[...], high) + dot(s[...], mid) + dot(s[...], low)

    def orthogonal(vectors, image, gram_cols, fresh, out):
        tile = jnp.where(lane8 == 0, correlate(vectors, image), 0.0)
        square = jnp.sum(jnp.sum(image * image, axis=0, keepdims=True), axis=1, keepdims=True)
        tile = tile + jnp.where(lane8 == 1, square, 0.0)
        if fresh is not None:
            tile = tile + fresh
        return tile

    def finish(vectors, image, total, gram_cols, out):
        c = total[:, 0:1]
        p2 = total[0:1, 1:2]
        gc = jnp.zeros((kb, 1), F32)
        part = image
        for k in range(kb):
            ck = c[k:k + 1, :]
            gc = gc + gram_cols[k] * ck
            part = part - ck * vectors[k][...]
        meansq = p2 + jnp.sum(c * gc - 2.0 * c * c, axis=0, keepdims=True)
        norm = jnp.sqrt(jnp.maximum(meansq, 0.0) + EPS)
        new = part * (1.0 / norm)
        out[...] = new
        return new, norm

    def shifted(cols, last):
        sub = lax.broadcasted_iota(jnp.int32, (kb, 1), 0)
        out = []
        for k in range(1, kb):
            moved = jnp.concatenate([cols[k][1:], last[k - 1:k]], axis=0)
            out.append(moved)
        return out + [last]

    norms = []
    for t in range(ITERS):
        wait_x()
        xp[...] = dot(pm[...], xr[t]).astype(BF16)
        products(xp, ps.at[t], False, t == 0)
        wait = rows_exchange("col", ps.at[t], pr.at[t])
        if t == 0:
            g = final()
            gram_r = [g[:, k:k + 1] for k in range(kb)]
            gram_l = [g[:, kb + k:kb + k + 1] for k in range(kb)]
            fresh_l = None
            fresh_r = None
        wait()
        image = scatter(sl, pr.at[t])
        total = all_reduce(orthogonal(left, image, gram_l, fresh_l, None))()()
        if fresh_l is not None:
            gram_l = shifted(gram_l, total[:, 2:3])
        new, alpha = finish(left, image, total, gram_l, nl.at[t])
        left = left[1:] + [nl.at[t]]
        zs[t] = dot(gl[...], new.astype(BF16)).astype(zs.dtype)
        wait = rows_exchange("col", zs.at[t], zr.at[t])
        if t + 1 < ITERS:
            fresh_l = jnp.where(lane8 == 2, correlate(left, new), 0.0)
        wait()
        xp[...] = dot(pmt[...], zr[t].astype(BF16)).astype(BF16)
        products(xp, qs.at[t], True, False)
        wait = rows_exchange("row", qs.at[t], qr.at[t])
        wait()
        image = scatter(sr, qr.at[t])
        total = all_reduce(orthogonal(right, image, gram_r, fresh_r, None))()()
        if fresh_r is not None:
            gram_r = shifted(gram_r, total[:, 2:3])
        new, beta = finish(right, image, total, gram_r, nr.at[t])
        right = right[1:] + [nr.at[t]]
        norms.append((alpha, beta))
        if t + 1 < ITERS:
            xs[t + 1] = dot(gr[...], new.astype(BF16)).astype(BF16)
            wait_x = rows_exchange("row", xs.at[t + 1], xr.at[t + 1])
            fresh_r = jnp.where(lane8 == 2, correlate(right, new), 0.0)

    r2 = lax.broadcasted_iota(jnp.int32, (2, ITERS), 0)
    c2 = lax.broadcasted_iota(jnp.int32, (2, ITERS), 1)
    value = jnp.zeros((2, ITERS), F32)
    for t in range(ITERS):
        for side in range(2):
            value = jnp.where((r2 == side) & (c2 == t), norms[t][side], value)
    bd[...] = value
    for copy in sends:
        copy.wait_send()


def solution(mesh):
    n_rows, n_cols = mesh.shape["row"], mesh.shape["col"]

    def body(tiles, rc, cc, lb, rb):
        _, _, slots, bs, _ = tiles.shape
        kb, own, _ = lb.shape
        wire = BF16 if (slots // n_cols) % 16 == 0 else F32
        reduces = 1 + 2 * ITERS
        vm = lambda shape, dtype: pltpu.VMEM(shape, dtype)
        col_phases = 1 + reduces + 2 * ITERS
        row_phases = 1 + reduces + 2 * ITERS
        ops = [pl.BlockSpec(memory_space=pl.ANY)] + [pl.BlockSpec(memory_space=pltpu.VMEM)] * 4
        return pl.pallas_call(
            functools.partial(kernel, n_rows, n_cols, slots, own, bs, kb),
            out_shape=(
                jax.ShapeDtypeStruct((ITERS, own, bs), F32),
                jax.ShapeDtypeStruct((ITERS, own, bs), F32),
                jax.ShapeDtypeStruct((2, ITERS), F32),
            ),
            in_specs=ops,
            out_specs=(pl.BlockSpec(memory_space=pltpu.VMEM),) * 3,
            scratch_shapes=[
                vm((slots, bs, bs), BF16),
                vm((slots, bs), wire), vm((slots, bs), wire),
                vm((slots, bs), BF16), vm((slots, bs), BF16),
                vm((slots, own), BF16), vm((own, slots), BF16),
                vm((slots, own), BF16), vm((own, slots), BF16),
                vm((slots, slots), BF16), vm((slots, slots), BF16),
                vm((ITERS, slots, bs), BF16), vm((ITERS, slots, bs), BF16),
                vm((ITERS, slots, bs), wire), vm((ITERS, slots, bs), wire),
                vm((ITERS, slots, bs), F32), vm((ITERS, slots, bs), F32),
                vm((ITERS, slots, bs), F32), vm((ITERS, slots, bs), F32),
                vm((slots, bs), BF16),
                vm((reduces, kb, bs), F32), vm((reduces, n_cols, kb, bs), F32),
                vm((reduces, kb, bs), F32), vm((reduces, n_rows, kb, bs), F32),
                pltpu.SemaphoreType.DMA((n_rows,)),
                pltpu.SemaphoreType.DMA((col_phases, n_cols)),
                pltpu.SemaphoreType.DMA((col_phases, n_cols)),
                pltpu.SemaphoreType.DMA((row_phases, n_rows)),
                pltpu.SemaphoreType.DMA((row_phases, n_rows)),
            ],
            compiler_params=pltpu.CompilerParams(
                collective_id=0, has_side_effects=True, vmem_limit_bytes=40 * 1024 * 1024
            ),
            name="lanczos",
        )(tiles, rc, cc, lb, rb)

    in_specs = (
        P("row", "col", None, None, None),
        P("row", "col", None),
        P("row", "col", None),
        P(None, ("row", "col"), None),
        P(None, ("col", "row"), None),
    )
    out_specs = (P(None, ("row", "col"), None), P(None, ("col", "row"), None), P())
    return jax.shard_map(body, mesh=mesh, in_specs=in_specs, out_specs=out_specs, check_vma=False)
```

profile of v0, /device:TPU:0, one launch (start us, length us, event | category | flops | bytes accessed | tf_op | source)
XLA Modules:
  0.0 107.3 jit_solution(16319998653446798691)
XLA Ops:
  0.6 0.0 copy-start
  0.6 1.2 %copy-done = f32[8,256,128]{2,1,0:T(8,128)S(1)} copy-done((f32[8,256,128]{2,1,0:T(8,128)S(1)}, f32[8,256,128]{2,1,0:T(8,128)}, u32[]{:S(2)}) %copy-start) | copy-done | bytes 1048600
  1.9 0.0 copy-start.1
  1.9 1.2 %copy-done.1 = f32[8,256,128]{2,1,0:T(8,128)S(1)} copy-done((f32[8,256,128]{2,1,0:T(8,128)S(1)}, f32[8,256,128]{2,1,0:T(8,128)}, u32[]{:S(2)}) %copy-start.1) | copy-done | bytes 1048600
  3.1 0.0 copy-start.2
  3.1 0.7 copy-done.2
  3.8 0.0 copy-start.3
  3.8 0.7 copy-done.3
  4.4 100.8 %lanczos.1 = (f32[2,256,128]{2,1,0:T(8,128)S(1)}, f32[2,256,128]{2,1,0:T(8,128)S(1)}, f32[2,2]{1,0:T(2,128)S(1)}) custom-call(bf16[1,1,384,128,128]{4,3,2,1,0:T(8,128)(2,1)} %tiles.1, s32[1,1,384]{2,1,0:T(1,128)S(1)} %copy-done.2, s32[1,1,384]{2,1,0:T(1,128)S(1)} %copy-done.3, f32[8,256,128]{2,1,0:T(8,128)S(1)} %copy-done, f32[8,256,128]{2,1,0:T(8,128)S(1)} %copy-done.1), custom_call_target="tpu_custom_call" | custom-call | tf_op jit(solution)/shard_map/lanczos/pallas_call | solution.py:303
  105.3 0.7 copy.11
  106.0 0.7 copy.12
  106.7 0.6 copy.13
Async XLA Ops:
  0.6 1.2 %copy-start = (f32[8,256,128]{2,1,0:T(8,128)S(1)}, f32[8,256,128]{2,1,0:T(8,128)}, u32[]{:S(2)}) copy-start(f32[8,256,128]{2,1,0:T(8,128)} %lb.1) | copy-start | bytes 3145732
  1.9 1.2 %copy-start.1 = (f32[8,256,128]{2,1,0:T(8,128)S(1)}, f32[8,256,128]{2,1,0:T(8,128)}, u32[]{:S(2)}) copy-start(f32[8,256,128]{2,1,0:T(8,128)} %rb.1) | copy-start | bytes 3145732
  3.1 0.7 copy-start.2
  3.8 0.7 copy-start.3
where the time goes:
time: 108 us; the launch traced here: 107 us
  Pallas kernels  101 us (94%)
  local copies, waits for them, and re-layouts  5.77 us (5%)
    pallas_call x1, Pallas kernels, body(): pl.pallas_call(functools.partial(kernel, n_rows, n_cols, slots, own, bs,...  101 us
    unnamed x11, local copies, waits for them, and re-layouts  5.77 us

commit v1 on v0

--- a/solution.py
+++ b/solution.py
@@ -25,11 +25,11 @@
 
 def kernel(
     n_rows, n_cols, slots, own, bs, kb,
-    tiles, rc, cc, lb, rb,
+    tiles, rc_h, cc_h, lb_h, rb_h,
     nl, nr, bd,
-    a_v, idl_s, idl_r, idr_s, idr_r, gl, sl, gr, sr, pm, pmt,
+    rc, cc, lb, rb, a_v, idl_s, idl_r, idr_s, idr_r, gl, sl, gr, sr, pm, pmt,
     xs, xr, zs, zr, ps, pr, qs, qr, xp, tc_s, tc_r, tr_s, tr_r,
-    a_sem, cs_sem, cr_sem, rs_sem, rr_sem,
+    in_sem, a_sem, cs_sem, cr_sem, rs_sem, rr_sem,
 ):
     i = lax.axis_index("row")
     j = lax.axis_index("col")
@@ -42,6 +42,12 @@
         part = pl.ds(b * rl, rl)
         return pltpu.make_async_copy(tiles.at[0, 0, part], a_v.at[part], a_sem.at[b])
 
+    inputs = [
+        pltpu.make_async_copy(src, dst, in_sem.at[k])
+        for k, (src, dst) in enumerate(((cc_h, cc), (rc_h, rc), (rb_h, rb), (lb_h, lb)))
+    ]
+    for copy in inputs:
+        copy.start()
     for b in range(n_rows):
         load(b).start()
 
@@ -93,8 +99,11 @@
 
     it0 = lax.broadcasted_iota(jnp.int32, (slots, slots), 0).astype(F32)
     it1 = lax.broadcasted_iota(jnp.int32, (slots, slots), 1).astype(F32)
-    pm[...] = jnp.where(place(it0) == it1, 1.0, 0.0).astype(BF16)
-    pmt[...] = jnp.where(place(it1) == it0, 1.0, 0.0).astype(BF16)
+    down = place(lax.broadcasted_iota(jnp.int32, (slots, 1), 0).astype(F32))
+    across = place(lax.broadcasted_iota(jnp.int32, (1, slots), 1).astype(F32))
+    pmt[...] = jnp.where(across == it0, 1.0, 0.0).astype(BF16)
+    inputs[0].wait()
+    inputs[1].wait()
 
     def column(row):
         return jnp.transpose(jnp.broadcast_to(row, (bs, slots)))
@@ -109,6 +118,9 @@
     pl.semaphore_wait(barrier, n_cols + n_rows - 2)
     wait_r = rows_exchange("row", idr_s, idr_r)
     wait_l = rows_exchange("col", idl_s, idl_r)
+
+    pm[...] = jnp.where(down == it1, 1.0, 0.0).astype(BF16)
+    inputs[2].wait()
 
     lane8 = lax.broadcasted_iota(jnp.int32, (kb, bs), 1)
 
@@ -150,6 +162,8 @@
 
     gram = jnp.zeros((kb, bs), F32)
     for side, vectors in enumerate((right, left)):
+        if side == 1:
+            inputs[3].wait()
         for l in range(kb):
             col = correlate(vectors, vectors[l][...])
             gram = gram + jnp.where(lane8 == side * kb + l, col, 0.0)
@@ -176,27 +190,60 @@
     final = middle()
     grams = None
 
-    row16 = lax.broadcasted_iota(jnp.int32, (16, bs), 0)
-
-    def products(x, out, transposed, first):
-        def body(b, carry):
-            if first:
-                load(b).wait()
-            for g in range(rl // 16):
-                part = pl.ds(pl.multiple_of(b * rl + g * 16, 16), 16)
-                xg = x[part, :].astype(F32)
-                acc = jnp.zeros((16, bs), F32)
-                for r in range(16):
-                    one = jnp.where(row16 == r, xg, 0.0).astype(BF16)
-                    k = g * 16 + r
-                    if transposed:
-                        t = k // cell * cl + b * cell + k % cell
-                        acc = acc + dot(one, a_v[t], NN)
-                    else:
-                        acc = acc + dot(one, a_v[b * rl + k], NT)
-                out[part, :] = acc
+    for b in range(n_rows):
+        load(b).wait()
+
+    def products(x, out, dst, axis):
+        me, n, ssem, rsem = axes[axis]
+        phase = used[axis]
+        used[axis] += 1
+        chunk = cl if axis == "col" else rl
+        group = 16 if chunk % 16 == 0 else 8
+        row_id = lax.broadcasted_iota(jnp.int32, (group, bs), 0)
+        mine = pl.ds(pl.multiple_of(me * chunk, chunk), chunk)
+
+        def copy(d):
+            peer = lax.rem(me + d, n)
+            return pltpu.make_async_remote_copy(
+                src_ref=out.at[pl.ds(pl.multiple_of(peer * chunk, chunk), chunk)], dst_ref=dst.at[mine],
+                send_sem=ssem.at[phase, d], recv_sem=rsem.at[phase, d],
+                device_id={axis: peer}, device_id_type=MESH,
+            )
+
+        def body(d, carry):
+            p = lax.rem(me + d, n)
+            for g in range(chunk // group):
+                part = pl.ds(pl.multiple_of(p * chunk + g * group, group), group)
+                xg = x[part, :]
+                lhs = jnp.concatenate(
+                    [jnp.where(row_id == r, xg, 0.0).astype(BF16) for r in range(group)], axis=1)
+                if axis == "col":
+                    rhs = a_v[pl.ds(p * chunk + g * group, group)].reshape(group * bs, bs)
+                else:
+                    ks = range(g * group, (g + 1) * group)
+                    rhs = jnp.concatenate([a_v[k // cell * cl + p * cell + k % cell] for k in ks], axis=0)
+                if axis == "col":
+                    o = dot(xg.astype(BF16), rhs, NT)
+                    acc = jnp.zeros((group, bs), F32)
+                    for r in range(group):
+                        acc = acc + jnp.where(row_id == r, o[:, r * bs:(r + 1) * bs], 0.0)
+                    out[part, :] = acc
+                else:
+                    out[part, :] = dot(lhs, rhs)
+
+            @pl.when(d < n)
+            def _():
+                copy(d).start()
             return carry
-        lax.fori_loop(0, n_rows, body, 0)
+        lax.fori_loop(1, n + 1, body, 0)
+        dst[mine, :] = out[mine, :]
+        copies = [copy(d) for d in range(1, n)]
+        sends.extend(copies)
+
+        def wait():
+            for c in copies:
+                c.wait_recv()
+        return wait
 
     def scatter(s, got):
         value = got[...]
@@ -206,13 +253,11 @@
         low = (rest - mid.astype(F32)).astype(BF16)
         return dot(s[...], high) + dot(s[...], mid) + dot(s[...], low)
 
-    def orthogonal(vectors, image, gram_cols, fresh, out):
+    def sums(vectors, image, fresh):
         tile = jnp.where(lane8 == 0, correlate(vectors, image), 0.0)
         square = jnp.sum(jnp.sum(image * image, axis=0, keepdims=True), axis=1, keepdims=True)
         tile = tile + jnp.where(lane8 == 1, square, 0.0)
-        if fresh is not None:
-            tile = tile + fresh
-        return tile
+        return tile if fresh is None else tile + fresh
 
     def finish(vectors, image, total, gram_cols, out):
         c = total[:, 0:1]
@@ -240,9 +285,8 @@
     norms = []
     for t in range(ITERS):
         wait_x()
-        xp[...] = dot(pm[...], xr[t]).astype(BF16)
-        products(xp, ps.at[t], False, t == 0)
-        wait = rows_exchange("col", ps.at[t], pr.at[t])
+        xp[...] = dot(pm[...], xr[t])
+        wait = products(xp, ps.at[t], pr.at[t], "col")
         if t == 0:
             g = final()
             gram_r = [g[:, k:k + 1] for k in range(kb)]
@@ -251,7 +295,7 @@
             fresh_r = None
         wait()
         image = scatter(sl, pr.at[t])
-        total = all_reduce(orthogonal(left, image, gram_l, fresh_l, None))()()
+        total = all_reduce(sums(left, image, fresh_l))()()
         if fresh_l is not None:
             gram_l = shifted(gram_l, total[:, 2:3])
         new, alpha = finish(left, image, total, gram_l, nl.at[t])
@@ -261,12 +305,11 @@
         if t + 1 < ITERS:
             fresh_l = jnp.where(lane8 == 2, correlate(left, new), 0.0)
         wait()
-        xp[...] = dot(pmt[...], zr[t].astype(BF16)).astype(BF16)
-        products(xp, qs.at[t], True, False)
-        wait = rows_exchange("row", qs.at[t], qr.at[t])
+        xp[...] = dot(pmt[...], zr[t].astype(BF16))
+        wait = products(xp, qs.at[t], qr.at[t], "row")
         wait()
         image = scatter(sr, qr.at[t])
-        total = all_reduce(orthogonal(right, image, gram_r, fresh_r, None))()()
+        total = all_reduce(sums(right, image, fresh_r))()()
         if fresh_r is not None:
             gram_r = shifted(gram_r, total[:, 2:3])
         new, beta = finish(right, image, total, gram_r, nr.at[t])
@@ -299,7 +342,7 @@
         vm = lambda shape, dtype: pltpu.VMEM(shape, dtype)
         col_phases = 1 + reduces + 2 * ITERS
         row_phases = 1 + reduces + 2 * ITERS
-        ops = [pl.BlockSpec(memory_space=pl.ANY)] + [pl.BlockSpec(memory_space=pltpu.VMEM)] * 4
+        ops = [pl.BlockSpec(memory_space=pl.ANY)] * 5
         return pl.pallas_call(
             functools.partial(kernel, n_rows, n_cols, slots, own, bs, kb),
             out_shape=(
@@ -310,6 +353,7 @@
             in_specs=ops,
             out_specs=(pl.BlockSpec(memory_space=pltpu.VMEM),) * 3,
             scratch_shapes=[
+                vm(rc.shape, jnp.int32), vm(cc.shape, jnp.int32), vm(lb.shape, F32), vm(rb.shape, F32),
                 vm((slots, bs, bs), BF16),
                 vm((slots, bs), wire), vm((slots, bs), wire),
                 vm((slots, bs), BF16), vm((slots, bs), BF16),
@@ -320,9 +364,10 @@
                 vm((ITERS, slots, bs), wire), vm((ITERS, slots, bs), wire),
                 vm((ITERS, slots, bs), F32), vm((ITERS, slots, bs), F32),
                 vm((ITERS, slots, bs), F32), vm((ITERS, slots, bs), F32),
-                vm((slots, bs), BF16),
+                vm((slots, bs), F32),
                 vm((reduces, kb, bs), F32), vm((reduces, n_cols, kb, bs), F32),
                 vm((reduces, kb, bs), F32), vm((reduces, n_rows, kb, bs), F32),
+                pltpu.SemaphoreType.DMA((4,)),
                 pltpu.SemaphoreType.DMA((n_rows,)),
                 pltpu.SemaphoreType.DMA((col_phases, n_cols)),
                 pltpu.SemaphoreType.DMA((col_phases, n_cols)),
@@ -330,7 +375,7 @@
                 pltpu.SemaphoreType.DMA((row_phases, n_rows)),
             ],
             compiler_params=pltpu.CompilerParams(
-                collective_id=0, has_side_effects=True, vmem_limit_bytes=40 * 1024 * 1024
+                collective_id=0, has_side_effects=True, vmem_limit_bytes=52 * 1024 * 1024
             ),
             name="lanczos",
         )(tiles, rc, cc, lb, rb)

time: 108 us -> 90.9 us (0.84)
  Pallas kernels: 101 us -> 85.5 us
  local copies, waits for them, and re-layouts: 5.77 us -> 4.55 us
    pallas_call x1, Pallas kernels: 101 us -> 85.5 us  [body(): pl.pallas_call(functools.partial(kernel, n_rows, n_cols, slots, own, bs,...]
    unnamed x11 -> x9, local copies, waits for them, and re-layouts: 5.77 us -> 4.55 us
where the time goes in v1:
time: 90.9 us; the launch traced here: 90.7 us
  Pallas kernels  85.5 us (94%)
  local copies, waits for them, and re-layouts  4.55 us (5%)
    pallas_call x1, Pallas kernels, body(): pl.pallas_call(functools.partial(kernel, n_rows, n_cols, slots, own, bs,...  85.5 us
    unnamed x9, local copies, waits for them, and re-layouts  4.55 us

profile of v1, /device:TPU:0, one launch (start us, length us, event | category | flops | bytes accessed | tf_op | source)
XLA Modules:
  0.0 90.7 jit_solution(16187246984411110324)
XLA Ops:
  0.6 0.0 copy-start
  0.6 1.2 %copy-done = f32[8,256,128]{2,1,0:T(8,128)S(1)} copy-done((f32[8,256,128]{2,1,0:T(8,128)S(1)}, f32[8,256,128]{2,1,0:T(8,128)}, u32[]{:S(2)}) %copy-start) | copy-done | bytes 1048600
  1.9 0.0 copy-start.1
  1.9 0.7 copy-done.1
  2.5 0.0 copy-start.2
  2.5 0.7 copy-done.2
  3.2 85.5 %lanczos.1 = (f32[2,256,128]{2,1,0:T(8,128)S(1)}, f32[2,256,128]{2,1,0:T(8,128)S(1)}, f32[2,2]{1,0:T(2,128)S(1)}) custom-call(bf16[1,1,384,128,128]{4,3,2,1,0:T(8,128)(2,1)} %tiles.1, s32[1,1,384]{2,1,0:T(1,128)S(1)} %copy-done.1, s32[1,1,384]{2,1,0:T(1,128)S(1)} %copy-done.2, f32[8,256,128]{2,1,0:T(8,128)S(1)} %copy-done, f32[8,256,128]{2,1,0:T(8,128)} %rb_h.1), custom_call_target="tpu_custom_call" | custom-call | tf_op jit(solution)/shard_map/lanczos/pallas_call | solution.py:346
  88.7 0.7 copy.11
  89.4 0.7 copy.12
  90.1 0.6 copy.13
Async XLA Ops:
  0.6 1.2 %copy-start = (f32[8,256,128]{2,1,0:T(8,128)S(1)}, f32[8,256,128]{2,1,0:T(8,128)}, u32[]{:S(2)}) copy-start(f32[8,256,128]{2,1,0:T(8,128)} %lb_h.1) | copy-start | bytes 3145732
  1.9 0.7 copy-start.1
  2.5 0.7 copy-start.2

commit v2 on v1

--- a/solution.py
+++ b/solution.py
@@ -29,7 +29,7 @@
     nl, nr, bd,
     rc, cc, lb, rb, a_v, idl_s, idl_r, idr_s, idr_r, gl, sl, gr, sr, pm, pmt,
     xs, xr, zs, zr, ps, pr, qs, qr, xp, tc_s, tc_r, tr_s, tr_r,
-    in_sem, a_sem, cs_sem, cr_sem, rs_sem, rr_sem,
+    in_sem, a_sem, cs_sem, cr_sem, rs_sem, rr_sem, as_sem, ar_sem,
 ):
     i = lax.axis_index("row")
     j = lax.axis_index("col")
@@ -52,14 +52,28 @@
         load(b).start()
 
     barrier = pltpu.get_barrier_semaphore()
-    for d in range(1, n_cols):
-        pl.semaphore_signal(barrier, inc=1, device_id={"col": lax.rem(j + d, n_cols)}, device_id_type=MESH)
-    for d in range(1, n_rows):
-        pl.semaphore_signal(barrier, inc=1, device_id={"row": lax.rem(i + d, n_rows)}, device_id_type=MESH)
+    n_all = n_rows * n_cols
+    me_all = i * n_cols + j
+    one_stage = n_all <= 32
+
+    def device(axis, me, d):
+        if axis == "all":
+            peer = lax.rem(me + d, n_all)
+            return {"row": peer // n_cols, "col": lax.rem(peer, n_cols)}
+        return {axis: lax.rem(me + d, n_cols if axis == "col" else n_rows)}
+
+    greeted = (("all", me_all, n_all),) if one_stage else (("col", j, n_cols), ("row", i, n_rows))
+    for axis, me, n in greeted:
+        for d in range(1, n):
+            pl.semaphore_signal(barrier, inc=1, device_id=device(axis, me, d), device_id_type=MESH)
 
     sends = []
-    axes = {"col": (j, n_cols, cs_sem, cr_sem), "row": (i, n_rows, rs_sem, rr_sem)}
-    used = {"col": 0, "row": 0}
+    axes = {
+        "col": (j, n_cols, cs_sem, cr_sem),
+        "row": (i, n_rows, rs_sem, rr_sem),
+        "all": (me_all, n_all, as_sem, ar_sem),
+    }
+    used = {"col": 0, "row": 0, "all": 0}
 
     def exchange(axis, src, dst):
         me, n, ssem, rsem = axes[axis]
@@ -71,7 +85,7 @@
             copy = pltpu.make_async_remote_copy(
                 src_ref=src(peer), dst_ref=dst(me),
                 send_sem=ssem.at[phase, d], recv_sem=rsem.at[phase, d],
-                device_id={axis: peer}, device_id_type=MESH,
+                device_id=device(axis, me, d), device_id_type=MESH,
             )
             copy.start()
             sends.append(copy)
@@ -115,7 +129,7 @@
     idl_s[...] = column(r_loc).astype(idl_s.dtype)
     idr_s[...] = dot(pmt[...], column(c_loc).astype(BF16)).astype(BF16)
 
-    pl.semaphore_wait(barrier, n_cols + n_rows - 2)
+    pl.semaphore_wait(barrier, n_all - 1 if one_stage else n_cols + n_rows - 2)
     wait_r = rows_exchange("row", idr_s, idr_r)
     wait_l = rows_exchange("col", idl_s, idl_r)
 
@@ -139,6 +153,14 @@
         n = all_reduce_count[0]
         all_reduce_count[0] += 1
         tc_s[n] = tile
+        if one_stage:
+            tr_r[n, me_all] = tile
+            wait_all = exchange("all", lambda p: tc_s.at[n], lambda p: tr_r.at[n, p])
+
+            def last():
+                wait_all()
+                return jnp.sum(tr_r[n], axis=0) * inverse
+            return lambda: last
         tc_r[n, j] = tile
         wait = exchange("col", lambda p: tc_s.at[n], lambda p: tc_r.at[n, p])
 
@@ -339,6 +361,8 @@
         kb, own, _ = lb.shape
         wire = BF16 if (slots // n_cols) % 16 == 0 else F32
         reduces = 1 + 2 * ITERS
+        n_all = n_rows * n_cols
+        one_stage = n_all <= 32
         vm = lambda shape, dtype: pltpu.VMEM(shape, dtype)
         col_phases = 1 + reduces + 2 * ITERS
         row_phases = 1 + reduces + 2 * ITERS
@@ -366,13 +390,15 @@
                 vm((ITERS, slots, bs), F32), vm((ITERS, slots, bs), F32),
                 vm((slots, bs), F32),
                 vm((reduces, kb, bs), F32), vm((reduces, n_cols, kb, bs), F32),
-                vm((reduces, kb, bs), F32), vm((reduces, n_rows, kb, bs), F32),
+                vm((reduces, kb, bs), F32), vm((reduces, n_all if one_stage else n_rows, kb, bs), F32),
                 pltpu.SemaphoreType.DMA((4,)),
                 pltpu.SemaphoreType.DMA((n_rows,)),
                 pltpu.SemaphoreType.DMA((col_phases, n_cols)),
                 pltpu.SemaphoreType.DMA((col_phases, n_cols)),
                 pltpu.SemaphoreType.DMA((row_phases, n_rows)),
                 pltpu.SemaphoreType.DMA((row_phases, n_rows)),
+                pltpu.SemaphoreType.DMA((reduces, n_all) if one_stage else (1, 1)),
+                pltpu.SemaphoreType.DMA((reduces, n_all) if one_stage else (1, 1)),
             ],
             compiler_params=pltpu.CompilerParams(
                 collective_id=0, has_side_effects=True, vmem_limit_bytes=52 * 1024 * 1024

time: 90.9 us -> 91 us (level)
  no operation moved by 1% of the time
where the time goes in v2:
time: 91 us; the launch traced here: 90.8 us
  Pallas kernels  85.6 us (94%)
  local copies, waits for them, and re-layouts  4.55 us (5%)
    pallas_call x1, Pallas kernels, body(): pl.pallas_call(functools.partial(kernel, n_rows, n_cols, slots, own, bs,...  85.6 us
    unnamed x9, local copies, waits for them, and re-layouts  4.55 us

profile of v2, /device:TPU:0, one launch (start us, length us, event | category | flops | bytes accessed | tf_op | source)
XLA Modules:
  0.0 90.8 jit_solution(2687120592762092782)
XLA Ops:
  0.6 0.0 copy-start
  0.6 1.2 %copy-done = f32[8,256,128]{2,1,0:T(8,128)S(1)} copy-done((f32[8,256,128]{2,1,0:T(8,128)S(1)}, f32[8,256,128]{2,1,0:T(8,128)}, u32[]{:S(2)}) %copy-start) | copy-done | bytes 1048600
  1.9 0.0 copy-start.1
  1.9 0.7 copy-done.1
  2.5 0.0 copy-start.2
  2.5 0.7 copy-done.2
  3.2 85.6 %lanczos.1 = (f32[2,256,128]{2,1,0:T(8,128)S(1)}, f32[2,256,128]{2,1,0:T(8,128)S(1)}, f32[2,2]{1,0:T(2,128)S(1)}) custom-call(bf16[1,1,384,128,128]{4,3,2,1,0:T(8,128)(2,1)} %tiles.1, s32[1,1,384]{2,1,0:T(1,128)S(1)} %copy-done.1, s32[1,1,384]{2,1,0:T(1,128)S(1)} %copy-done.2, f32[8,256,128]{2,1,0:T(8,128)S(1)} %copy-done, f32[8,256,128]{2,1,0:T(8,128)} %rb_h.1), custom_call_target="tpu_custom_call" | custom-call | tf_op jit(solution)/shard_map/lanczos/pallas_call | solution.py:370
  88.8 0.7 copy.11
  89.5 0.7 copy.12
  90.2 0.6 copy.13
Async XLA Ops:
  0.6 1.2 %copy-start = (f32[8,256,128]{2,1,0:T(8,128)S(1)}, f32[8,256,128]{2,1,0:T(8,128)}, u32[]{:S(2)}) copy-start(f32[8,256,128]{2,1,0:T(8,128)} %lb_h.1) | copy-start | bytes 3145732
  1.9 0.7 copy-start.1
  2.5 0.7 copy-start.2
